TPU v7x, 512 devices: a whole 4x8x8 slice. The times are simulated.
512 devices in a mesh: recv: 64 (over z, y_hi, core), win: 8 (over x, y_lo).
Axes of the slice: x: 4, y: 8 (y_hi: 4, y_lo: 2; y = y_hi * 2 + y_lo), z: 8, core: 2. Of those that a mesh axis runs over, the one named last changes fastest.
Arguments:
- spectra: float32 [8, 256, 2, 4352], P('win', 'recv'), may hold values from -6 to 6
- sources: int32 [16], replicated, may hold values from 0 to 255
Outputs:
- correlograms: float32 [16, 256, 1001], P('win', 'recv')
All inputs are finite; a program needn't handle non-finite values.
Results may differ from a plain program's by a relative error of at most 0.0001.
Values sent between devices are 32-bit elements; how exact they have to be, the bound alone decides.
A program may use at most 64 MiB of HBM per device.

v0:
```python
import math

import jax
import jax.numpy as jnp
from jax import lax
from jax.sharding import PartitionSpec as P

BINS = 4352
NFFT = 16384
FIRST = 256
HALF = 500


def whiten(spectra):
    power = jnp.sum(spectra * spectra, axis=(-2, -1), keepdims=True) / spectra.shape[-1]
    return spectra * lax.rsqrt(power + 1e-06)


def lag_table(start, width, windows):
    freqs = FIRST + start + jnp.arange(width, dtype=jnp.int32)
    shifts = jnp.arange(2 * HALF + 1, dtype=jnp.int32) - HALF
    phase = (freqs[:, None] * shifts[None, :] % NFFT).astype(jnp.float32) * (2.0 * math.pi / NFFT)
    bins_at = (start + jnp.arange(width, dtype=jnp.int32)).astype(jnp.float32)
    taper = jnp.sin(math.pi * (bins_at + 0.5) / BINS) / jnp.sqrt(jnp.float32(windows * BINS))
    return (jnp.cos(phase) * taper[:, None], -jnp.sin(phase) * taper[:, None])


def inverse_lags(real_part, imag_part, windows):
    lead = real_part.shape[:-1]
    nbins = real_part.shape[-1]
    real_rows = real_part.reshape(-1, nbins)
    imag_rows = imag_part.reshape(-1, nbins)
    width = math.gcd(nbins, 256)

    def step(index, total):
        start = (index * width).astype(jnp.int32)
        cosines, sines = lag_table(start, width, windows)
        left = lax.dynamic_slice_in_dim(real_rows, start, width, 1)
        right = lax.dynamic_slice_in_dim(imag_rows, start, width, 1)
        total = total + jnp.dot(left, cosines, precision=lax.Precision.HIGHEST)
        return total + jnp.dot(right, sines, precision=lax.Precision.HIGHEST)

    empty = jnp.zeros((real_rows.shape[0], 2 * HALF + 1), jnp.float32)
    total = lax.fori_loop(0, nbins // width, step, empty)
    return total.reshape(lead + (2 * HALF + 1,))


def shards(spectra, sources):
    white = whiten(spectra)[0]
    chan_dev = white.shape[0]
    nbins = white.shape[2]
    nsrc = sources.shape[0]
    windows = lax.axis_size("win")
    owned = lax.axis_index("recv") * chan_dev + jnp.arange(chan_dev, dtype=jnp.int32)
    onehot = (sources[:, None] == owned[None, :]).astype(jnp.float32)
    local = jnp.dot(onehot, white.reshape(chan_dev, 2 * nbins), precision=lax.Precision.HIGHEST)
    source = lax.psum(local, "recv").reshape(nsrc, 2, nbins)
    cross_re = source[:, None, 0] * white[None, :, 0] + source[:, None, 1] * white[None, :, 1]
    cross_im = source[:, None, 1] * white[None, :, 0] - source[:, None, 0] * white[None, :, 1]
    stacked = lax.psum_scatter(
        jnp.stack([cross_re, cross_im], 2), "win", scatter_dimension=0, tiled=True
    )
    return inverse_lags(stacked[:, :, 0], stacked[:, :, 1], windows)


def solution(mesh):
    in_specs = (P("win", "recv", None, None), P())
    out_specs = P("win", "recv", None)
    return jax.shard_map(shards, mesh=mesh, in_specs=in_specs, out_specs=out_specs, check_vma=False)
```

profile of v0, /device:TPU:1, one launch (start us, length us, event | category | flops | bytes accessed | tf_op | source)
XLA Modules:
  0.0 818.9 jit_solution(14912824616010544861)
XLA Ops:
  11.2 522.5 %all-reduce.4.cloned.1.call-done = f32[16,2,4352]{2,1,0:T(2,128)} async-done(((f32[16,2,4352]{2,1,0:T(2,128)}), f32[16,2,4352]{2,1,0:T(2,128)}) %all-reduce.4.cloned.1.call-update) | async-done | bytes 557072 | tf_op jit(solution)/shard_map/psum | solution.py:57
  539.8 115.1 %all-reduce.6.cloned.1.call-done = f32[16,4,2,4352]{3,1,0,2:T(4,128)} async-done(((f32[16,4,2,4352]{3,1,0,2:T(4,128)}), f32[16,4,2,4352]{3,1,0,2:T(4,128)}) %all-reduce.6.cloned.1.call-update) | async-done | bytes 2228240
  656.0 155.4 %while.16 = (s32[]{:T(128)}, f32[8,1001]{1,0:T(8,128)S(1)}, f32[8,4352]{1,0:T(8,128)S(1)}, f32[8,4352]{1,0:T(8,128)S(1)}, s32[]{:T(128)}, /*index=5*/s32[]{:T(128)}, s32[]{:T(128)}, s32[]{:T(128)}) while((s32[]{:T(128)}, f32[8,1001]{1,0:T(8,128)S(1)}, f32[8,4352]{1,0:T(8,128)S(1)}, f32[8,4352]{1,0:T(8,128)S(1)}, s32[]{:T(128)}, ...), condition=%wide.region_4.5_spmd.clone, body=%wide.region_3.4_spmd.clone.sunk | while | flops 57171656 | bytes 164493 | solution.py:44
  660.6 4.6 convolution_add_fusion.5
  665.2 4.5 convolution_add_fusion.4
  669.7 4.6 convolution_add_fusion.5
  678.9 4.6 convolution_add_fusion.5
  688.0 4.6 convolution_add_fusion.5
  692.7 4.5 convolution_add_fusion.4
  697.2 4.6 convolution_add_fusion.5
  706.3 4.6 convolution_add_fusion.5
  715.4 4.6 convolution_add_fusion.5
  720.1 4.5 convolution_add_fusion.4
  724.6 4.6 convolution_add_fusion.5
  733.7 4.6 convolution_add_fusion.5
  742.9 4.6 convolution_add_fusion.5
  747.5 4.5 convolution_add_fusion.4
  752.0 4.6 convolution_add_fusion.5
  761.1 4.6 convolution_add_fusion.5
  770.3 4.6 convolution_add_fusion.5
  779.4 4.6 convolution_add_fusion.5
  788.5 4.6 convolution_add_fusion.5
  797.7 4.6 convolution_add_fusion.5
  806.8 4.6 convolution_add_fusion.5
  (87 shorter events, 71.1 us)
Async XLA Ops:
  6.5 527.2 %all-reduce.4.cloned.1.call-start = ((), (), s32[]{:S(2)}) async-start(), calls=%async_computation | async-start | bytes 1114112 | tf_op jit(solution)/shard_map/psum | solution.py:57
  11.0 643.9 %all-reduce.6.cloned.1.call-start = ((), (), s32[]{:S(2)}) async-start(), calls=%async_computation.1 | async-start | bytes 4456448
Sparse Core Ops, SparseCore 0:
  11.1 522.5 all-reduce.3
  537.9 116.9 all-reduce.5
where the time goes:
time: 819 us
  waiting for transfers between devices  638 us (78%)
  matrix products  155 us (19%)
  between operations  14.2 us (2%)
    psum x1, waiting for transfers between devices, shards(): source = lax.psum(local, 'recv').reshape(nsrc, 2, nbins)  522 us
    unnamed x3, waiting for transfers between devices  115 us
    dot_general x17, matrix products, step(): return total + jnp.dot(right, sines, precision=lax.Precision.HIGHEST)  77.7 us
    dot_general x17, matrix products, step(): total = total + jnp.dot(left, cosines, precision=lax.Precision.HIGHEST)  76.5 us
  transfers between devices with their start and end apart: 2, of which 2 were waited for; matrix products, arithmetic and copies ran while one was open for 0% of the time, Pallas kernels for 0%

commit v1 on v0

v1 whole, which is shorter than its diff:
```python
import math

import jax
import jax.numpy as jnp
import numpy as np
from jax import lax
from jax.experimental import pallas as pl
from jax.experimental.pallas import tpu as pltpu
from jax.sharding import PartitionSpec as P

BINS = 4352
NFFT = 16384
FIRST = 256
HALF = 500
LAGS = 2 * HALF + 1
NSRC = 16
WINDOWS = 8
CHAN = 4
DEPTH = 8
ROWS = 4
RECV = 64
TILES = BINS // 128
OWN = 4
LEFT = TILES - OWN * WINDOWS
WORK = OWN + LEFT
WIDE = 1024
CUT = 256
CUTS = WIDE // CUT
ITEMS = WINDOWS * OWN + LEFT
MESH = pl.DeviceIdType.MESH
F32 = jnp.float32
BF16 = jnp.bfloat16


def tables():
    lags = np.arange(WIDE, dtype=np.int64) - HALF
    turn = 2.0 * np.pi / NFFT
    inner = (np.arange(128)[:, None] * lags[None, :]) % NFFT * turn
    base = np.concatenate([np.cos(inner), np.sin(inner)]).astype(np.float32)
    first = FIRST + 128 * np.arange(TILES, dtype=np.int64)
    outer = (first[:, None] * lags[None, :]) % NFFT * turn
    rot = np.zeros((TILES, 8, WIDE), np.float32)
    rot[:, 0] = np.cos(outer)
    rot[:, 1] = np.sin(outer)
    taper = np.sin(np.pi * (np.arange(BINS) + 0.5) / BINS) / math.sqrt(WINDOWS * BINS)
    rot[:, 2, :128] = taper.reshape(TILES, 128)
    return base, rot


def kernel(
    spec_hbm, src, base_hbm, rot_hbm, out,
    spec, white, heard, chans, items, base, rot, thi, tlo, cross, part, parts,
    load_sem, own_sem, hear_send, hear_recv, chan_send, chan_recv, item_send, item_recv, part_send, part_recv,
):
    r = lax.axis_index("recv")
    w = lax.axis_index("win")
    core = lax.rem(r, 2)
    y = lax.rem(lax.div(r, 2), ROWS)
    z = lax.div(r, 2 * ROWS)

    def at(z2, y2, core2):
        return (z2 * ROWS + y2) * 2 + core2

    regular = core == lax.rem(y, 2)
    left = (z == w) & (((y == 0) & (core == 1)) | ((y == 1) & (core == 0)))
    holder = regular | left
    mine = jnp.where(regular, z * OWN + y, WINDOWS * OWN + jnp.where(core == 0, 1, 0))

    loads = [
        pltpu.make_async_copy(spec_hbm, spec, load_sem.at[0]),
        pltpu.make_async_copy(base_hbm, base, load_sem.at[1]),
        pltpu.make_async_copy(rot_hbm.at[pl.ds(OWN * w, OWN)], rot.at[pl.ds(0, OWN)], load_sem.at[2]),
        pltpu.make_async_copy(rot_hbm.at[pl.ds(OWN * WINDOWS, LEFT)], rot.at[pl.ds(OWN, LEFT)], load_sem.at[3]),
    ]
    for load in loads:
        load.start()

    barrier = pltpu.get_barrier_semaphore()

    def greet(r2, w2):
        pl.semaphore_signal(barrier, inc=1, device_id=(r2, w2), device_id_type=MESH)

    @pl.when(holder)
    def _():
        def one(r2, carry):
            @pl.when((r2 != r) | (z != w))
            def _():
                greet(r2, z)

            return carry

        lax.fori_loop(0, RECV, one, 0)

    def others(size, me):
        return [lax.rem(me + d, size) for d in range(1, size)]

    for w2 in others(WINDOWS, w):
        greet(r, w2)
    for z2 in others(DEPTH, z):
        greet(at(z2, y, core), w)
    for y2 in others(ROWS, y):
        greet(at(z, y2, core), w)
    greet(at(z, y, 1 - core), w)

    loads[0].wait()
    for c in range(CHAN):
        both = spec[0, c]
        power = jnp.sum(both * both, axis=(0, 1), keepdims=True) / BINS
        both = both * lax.rsqrt(power + 1e-06)
        for t in range(TILES):
            white[t, c : c + 1, :] = both[0:1, 128 * t : 128 * t + 128]
            white[t, CHAN + c : CHAN + c + 1, :] = both[1:2, 128 * t : 128 * t + 128]

    own_chans = pltpu.make_async_copy(white.at[pl.ds(OWN * w, OWN)], chans.at[w], own_sem.at[0])
    own_chans.start()

    self_held = holder & (z == w)
    pl.semaphore_wait(barrier, jnp.where(self_held, TILES - 1, TILES) + 7 + 7 + 3 + 1)

    def tell(i, carry):
        t = lax.rem(i + r, TILES)
        q = lax.rem(t, OWN)
        in_col = t < OWN * WINDOWS
        w2 = jnp.where(in_col, lax.div(t, OWN), w)
        r2 = jnp.where(in_col, at(w, q, lax.rem(q, 2)), jnp.where(t == OWN * WINDOWS, at(w, 0, 1), at(w, 1, 0)))
        self = (r2 == r) & (w2 == w)

        @pl.when(self)
        def _():
            pltpu.make_async_copy(white.at[t], heard.at[r], hear_recv).start()

        @pl.when(jnp.logical_not(self))
        def _():
            pltpu.make_async_remote_copy(
                white.at[t], heard.at[r], hear_send, hear_recv, device_id=(r2, w2), device_id_type=MESH
            ).start()

        return carry

    lax.fori_loop(0, TILES, tell, 0)
    for w2 in others(WINDOWS, w):
        pltpu.make_async_remote_copy(
            white.at[pl.ds(OWN * w2, OWN)], chans.at[w], chan_send, chan_recv, device_id=(r, w2), device_id_type=MESH
        ).start()

    for load in loads[1:]:
        load.wait()

    def table(i, carry):
        u = lax.div(i, 8)
        row = pl.multiple_of(lax.rem(i, 8) * 16, 16)
        ct = rot[u, 0:1, :]
        st = rot[u, 1:2, :]
        cb = base[pl.ds(row, 16), :]
        sb = base[pl.ds(row + 128, 16), :]
        at_re = pl.multiple_of(u * 256 + row, 16)
        for value, place in ((cb * ct - sb * st, at_re), (-(sb * ct + cb * st), at_re + 128)):
            high = value.astype(BF16)
            thi[pl.ds(place, 16), :] = high
            tlo[pl.ds(place, 16), :] = (value - high.astype(F32)).astype(BF16)
        return carry

    lax.fori_loop(0, WORK * 8, table, 0)

    def send_item(i, r2):
        pltpu.make_async_remote_copy(
            items.at[i], items.at[i], item_send.at[i], item_recv.at[i], device_id=(r2, w), device_id_type=MESH
        ).start()

    def await_item(i):
        pltpu.make_async_copy(items.at[i], items.at[i], item_recv.at[i]).wait()

    def to_core(i):
        send_item(i, at(z, y, 1 - core))

    def to_rows(i):
        for y2 in others(ROWS, y):
            send_item(i, at(z, y2, core))

    def to_depth(i):
        for z2 in others(DEPTH, z):
            send_item(i, at(z2, y, core))

    @pl.when(holder)
    def _():
        pltpu.make_async_copy(heard, heard, hear_recv).wait()
        for k in range(NSRC):
            s = src[k]
            d = lax.shift_right_logical(s, 2)
            c = lax.bitwise_and(s, 3)
            items[mine, k : k + 1, :] = heard[d, pl.ds(c, 1), :]
            items[mine, NSRC + k : NSRC + k + 1, :] = heard[d, pl.ds(c + CHAN, 1), :]

    spare = WINDOWS * OWN

    @pl.when(core == 0)
    def _():
        @pl.when(holder)
        def _():
            to_rows(mine)
            to_depth(mine)
            to_core(mine)

        for q in (0, 2):

            @pl.when(y != q)
            def _():
                await_item(z * OWN + q)
                to_depth(z * OWN + q)
                to_core(z * OWN + q)

        @pl.when((z == w) & (y != 1))
        def _():
            await_item(spare + 1)
            to_depth(spare + 1)
            to_core(spare + 1)

        for z2 in others(DEPTH, z):
            for q in (0, 2):
                await_item(z2 * OWN + q)
                to_core(z2 * OWN + q)

        @pl.when(z != w)
        def _():
            await_item(spare + 1)
            to_core(spare + 1)

        for z2 in range(DEPTH):
            for q in (1, 3):
                await_item(z2 * OWN + q)
        await_item(spare)

    @pl.when(core == 1)
    def _():
        @pl.when(holder)
        def _():
            to_depth(mine)
            to_rows(mine)
            to_core(mine)

        @pl.when(regular)
        def _():
            for z2 in others(DEPTH, z):
                await_item(z2 * OWN + y)
                to_rows(z2 * OWN + y)
                to_core(z2 * OWN + y)

        @pl.when((y == 0) & (z != w))
        def _():
            await_item(spare)
            to_rows(spare)
            to_core(spare)

        for q in (1, 3):

            @pl.when(y != q)
            def _():
                for z2 in range(DEPTH):
                    await_item(z2 * OWN + q)
                    to_core(z2 * OWN + q)

        @pl.when(y != 0)
        def _():
            await_item(spare)
            to_core(spare)

        for z2 in range(DEPTH):
            for q in (0, 2):
                await_item(z2 * OWN + q)
        await_item(spare + 1)

    own_chans.wait()
    for _w2 in range(1):
        pltpu.make_async_copy(chans.at[pl.ds(0, 7)], chans.at[pl.ds(0, 7)], chan_recv).wait()

    upper = lax.broadcasted_iota(jnp.int32, (8, 128), 0) < CHAN

    def add(total, chan, i):
        turned = pltpu.roll(chan, CHAN, 0)
        plus = jnp.where(upper, chan, -chan)
        return tuple(
            total[k] + items[i, k : k + 1, :] * plus + items[i, NSRC + k : NSRC + k + 1, :] * turned
            for k in range(NSRC)
        )

    def put(u, total):
        taper = rot[u, 2:3, 0:128]
        col = pl.multiple_of(u * 256, 256)
        for p in range(NSRC // 4):
            halves = []
            for g in (2 * p, 2 * p + 1):
                a, b = total[2 * g], total[2 * g + 1]
                re = jnp.where(upper, a, pltpu.roll(b, CHAN, 0)) * taper
                im = jnp.where(upper, pltpu.roll(a, CHAN, 0), b) * taper
                halves.append((re, im))
            for j in range(2):
                value = jnp.concatenate([halves[0][j], halves[1][j]], axis=0)
                high = value.astype(BF16)
                cross[16 * p : 16 * p + 16, pl.ds(col + 128 * j, 128)] = high
                cross[64 + 16 * p : 64 + 16 * p + 16, pl.ds(col + 128 * j, 128)] = (
                    value - high.astype(F32)
                ).astype(BF16)

    nothing = tuple(jnp.zeros((8, 128), F32) for _ in range(NSRC))

    def tile(q, carry):
        put(q, lax.fori_loop(0, WINDOWS, lambda v, total: add(total, chans[v, q], v * OWN + q), nothing))
        return carry

    lax.fori_loop(0, OWN, tile, 0)

    def tail(j, carry):
        put(OWN + j, add(nothing, white[spare + j], spare + j))
        return carry

    lax.fori_loop(0, LEFT, tail, 0)

    for n in range(CUTS):
        cols = slice(CUT * n, CUT * n + CUT)
        both = jnp.dot(cross[...], thi[:, cols], preferred_element_type=F32)
        low = jnp.dot(cross[0:64, :], tlo[:, cols], preferred_element_type=F32)
        value = both[0:64] + both[64:128] + low
        for g in range(WINDOWS):
            part[n * WINDOWS + g] = value[8 * g : 8 * g + 8]
        pltpu.make_async_copy(part.at[n * WINDOWS + w], parts.at[w, n], own_sem.at[1]).start()
        for w2 in others(WINDOWS, w):
            pltpu.make_async_remote_copy(
                part.at[n * WINDOWS + w2], parts.at[w, n], part_send, part_recv, device_id=(r, w2), device_id_type=MESH
            ).start()

    pltpu.make_async_copy(parts.at[0], parts.at[0], own_sem.at[1]).wait()
    pltpu.make_async_copy(parts.at[pl.ds(0, 7)], parts.at[pl.ds(0, 7)], part_recv).wait()
    for n in range(CUTS):
        width = min(CUT, LAGS - CUT * n)
        total = parts[0, n]
        for v in range(1, WINDOWS):
            total = total + parts[v, n]
        for k in range(2):
            out[k, :, CUT * n : CUT * n + width] = total[CHAN * k : CHAN * k + CHAN, 0:width]

    many = pl.ds(0, WORK + 1)
    pltpu.make_async_copy(chans.at[pl.ds(0, 7)], chans.at[pl.ds(0, 7)], chan_send).wait()
    pltpu.make_async_copy(part.at[pl.ds(0, 7 * CUTS)], part.at[pl.ds(0, 7 * CUTS)], part_send).wait()

    @pl.when(self_held)
    def _():
        pltpu.make_async_copy(white.at[pl.ds(0, TILES - 1)], white.at[pl.ds(0, TILES - 1)], hear_send).wait()

    @pl.when(jnp.logical_not(self_held))
    def _():
        pltpu.make_async_copy(white, white, hear_send).wait()

    def sent(i, count):
        pltpu.make_async_copy(items.at[pl.ds(0, count)], items.at[pl.ds(0, count)], item_send.at[i]).wait()

    @pl.when(holder)
    def _():
        sent(mine, 11)

    @pl.when(core == 0)
    def _():
        for q in (0, 2):

            @pl.when(y != q)
            def _():
                sent(z * OWN + q, 8)

        @pl.when((z == w) & (y != 1))
        def _():
            sent(spare + 1, 8)

        for z2 in others(DEPTH, z):
            for q in (0, 2):
                sent(z2 * OWN + q, 1)

        @pl.when(z != w)
        def _():
            sent(spare + 1, 1)

    @pl.when(core == 1)
    def _():
        @pl.when(regular)
        def _():
            for z2 in others(DEPTH, z):
                sent(z2 * OWN + y, 4)

        @pl.when((y == 0) & (z != w))
        def _():
            sent(spare, 4)

        for q in (1, 3):

            @pl.when(y != q)
            def _():
                for z2 in range(DEPTH):
                    sent(z2 * OWN + q, 1)

        @pl.when(y != 0)
        def _():
            sent(spare, 1)


def shards(spectra, sources):
    base, rot = tables()
    anywhere = pl.BlockSpec(memory_space=pl.ANY)
    vmem = pltpu.VMEM
    dma = pltpu.SemaphoreType.DMA
    return pl.pallas_call(
        kernel,
        out_shape=jax.ShapeDtypeStruct((NSRC // WINDOWS, CHAN, LAGS), F32),
        in_specs=[anywhere, pl.BlockSpec(memory_space=pltpu.SMEM), anywhere, anywhere],
        out_specs=pl.BlockSpec(memory_space=vmem),
        scratch_shapes=[
            vmem((1, CHAN, 2, BINS), F32),
            vmem((TILES, 8, 128), F32),
            vmem((RECV, 8, 128), F32),
            vmem((WINDOWS, OWN, 8, 128), F32),
            vmem((ITEMS, 2 * NSRC, 128), F32),
            vmem((256, WIDE), F32),
            vmem((WORK, 8, WIDE), F32),
            vmem((WORK * 256, WIDE), BF16),
            vmem((WORK * 256, WIDE), BF16),
            vmem((128, WORK * 256), BF16),
            vmem((CUTS * WINDOWS, 8, CUT), F32),
            vmem((WINDOWS, CUTS, 8, CUT), F32),
            dma((4,)),
            dma((2,)),
            dma,
            dma,
            dma,
            dma,
            dma((ITEMS,)),
            dma((ITEMS,)),
            dma,
            dma,
        ],
        compiler_params=pltpu.CompilerParams(
            collective_id=0, has_side_effects=True, vmem_limit_bytes=32 * 1024 * 1024
        ),
    )(spectra, sources, jnp.asarray(base), jnp.asarray(rot))


def solution(mesh):
    in_specs = (P("win", "recv", None, None), P())
    out_specs = P("win", "recv", None)
    return jax.shard_map(shards, mesh=mesh, in_specs=in_specs, out_specs=out_specs, check_vma=False)
```

time: 819 us -> 52.8 us (0.06)
  waiting for transfers between devices: 638 us -> 0 us
  matrix products: 155 us -> 0 us
  Pallas kernels: 0 us -> 48 us
  between operations: 14.2 us -> 0.01 us
    psum x1 -> x0, waiting for transfers between devices: 522 us -> none  [shards(): source = lax.psum(local, 'recv').reshape(nsrc, 2, nbins)]
    dot_general x35 -> x0, matrix products: 155 us -> none  [the longest x17 77.7 us: step(): return total + jnp.dot(right, sines, precision=lax.Precision.HIGHEST)]
    unnamed x3 -> x0, waiting for transfers between devices: 115 us -> none
    pallas_call x0 -> x1, Pallas kernels: none -> 48 us  [shards(): pl.pallas_call(kernel, out_shape=jax.ShapeDtypeStruct((NSRC // WINDOWS, C...]
  transfers between devices with their start and end apart: 2 -> 0, of which waited for: 2 -> 0; matrix products, arithmetic and copies ran while one was open for 0% -> 0% of each run, Pallas kernels for 0% -> 0%
where the time goes in v1:
time: 52.8 us; the launch traced here: 52.6 us
  Pallas kernels  48 us (91%)
  local copies, waits for them, and re-layouts  4.65 us (9%)
    pallas_call x1, Pallas kernels, shards(): pl.pallas_call(kernel, out_shape=jax.ShapeDtypeStruct((NSRC // WINDOWS, C...  48 us
    unnamed x9, local copies, waits for them, and re-layouts  4.65 us

profile of v1, /device:TPU:1, one launch (start us, length us, event | category | flops | bytes accessed | tf_op | source)
XLA Modules:
  0.0 52.6 jit_solution(4772415200619595120)
XLA Ops:
  0.0 0.0 copy-start
  0.0 1.2 %copy-done = f32[34,8,1024]{2,1,0:T(8,128)S(1)} copy-done((f32[34,8,1024]{2,1,0:T(8,128)S(1)}, f32[34,8,1024]{2,1,0:T(8,128)}, u32[]{:S(2)}) %copy-start) | copy-done | bytes 1114136
  1.2 0.0 copy-start.1
  1.3 1.2 %copy-done.1 = f32[256,1024]{1,0:T(8,128)S(1)} copy-done((f32[256,1024]{1,0:T(8,128)S(1)}, f32[256,1024]{1,0:T(8,128)}, u32[]{:S(2)}) %copy-start.1) | copy-done | bytes 1048600
  2.5 0.0 copy-start.2
  2.5 0.9 %copy-done.2 = f32[1,4,2,4352]{3,2,1,0:T(2,128)S(1)} copy-done((f32[1,4,2,4352]{3,2,1,0:T(2,128)S(1)}, f32[1,4,2,4352]{3,2,1,0:T(2,128)}, u32[]{:S(2)}) %copy-start.2) | copy-done | bytes 139288
  3.4 0.0 copy-start.3
  3.4 0.7 %copy-done.3 = s32[16]{0:T(128)S(1)} copy-done((s32[16]{0:T(128)S(1)}, s32[16]{0:T(128)}, u32[]{:S(2)}) %copy-start.3) | copy-done | bytes 88
  4.0 48.0 %shard_map.46 = f32[2,4,1001]{2,1,0:T(4,128)S(1)} custom-call(f32[1,4,2,4352]{3,2,1,0:T(2,128)S(1)} %copy-done.2, s32[16]{0:T(128)S(1)} %copy-done.3, f32[256,1024]{1,0:T(8,128)S(1)} %copy-done.1, f32[34,8,1024]{2,1,0:T(8,128)S(1)} %copy-done), custom_call_target="tpu_custom_call" | custom-call | tf_op jit(solution)/shard_map/pallas_call | solution.py:408
  52.0 0.6 %copy.6 = f32[2,4,1001]{2,1,0:T(4,128)} copy(f32[2,4,1001]{2,1,0:T(4,128)S(1)} %shard_map.46) | data formatting | bytes 64064
Async XLA Ops:
  0.0 1.2 %copy-start = (f32[34,8,1024]{2,1,0:T(8,128)S(1)}, f32[34,8,1024]{2,1,0:T(8,128)}, u32[]{:S(2)}) copy-start(f32[34,8,1024]{2,1,0:T(8,128)} %constant.5.clone.rot_hbm) | copy-start | bytes 3342340
  1.2 1.2 %copy-start.1 = (f32[256,1024]{1,0:T(8,128)S(1)}, f32[256,1024]{1,0:T(8,128)}, u32[]{:S(2)}) copy-start(f32[256,1024]{1,0:T(8,128)} %constant.4.clone.base_hbm) | copy-start | bytes 3145732
  2.5 0.9 %copy-start.2 = (f32[1,4,2,4352]{3,2,1,0:T(2,128)S(1)}, f32[1,4,2,4352]{3,2,1,0:T(2,128)}, u32[]{:S(2)}) copy-start(f32[1,4,2,4352]{3,2,1,0:T(2,128)} %spec_hbm.1) | copy-start | bytes 417796
  3.4 0.7 %copy-start.3 = (s32[16]{0:T(128)S(1)}, s32[16]{0:T(128)}, u32[]{:S(2)}) copy-start(s32[16]{0:T(128)} %src.1) | copy-start | bytes 196

commit v2 on v0

v2 whole, which is shorter than its diff:
```python
import math

import jax
import jax.numpy as jnp
import numpy as np
from jax import lax
from jax.experimental import pallas as pl
from jax.experimental.pallas import tpu as pltpu
from jax.sharding import PartitionSpec as P

BINS = 4352
NFFT = 16384
FIRST = 256
HALF = 500
LAGS = 2 * HALF + 1
NSRC = 16
WINDOWS = 8
CHAN = 4
ROWS = 4
RECV = 64
TILES = BINS // 128
ITEMS = TILES + 1
PART = NSRC // 2
WIDE = 512
CUT = 256
GROUP = 17
FIRST_PART = 17
MARKER = 21
SPARE = RECV // 2
MESH = pl.DeviceIdType.MESH
F32 = jnp.float32
BF16 = jnp.bfloat16


def tables():
    lags = np.arange(WIDE, dtype=np.int64)
    turn = 2.0 * np.pi / NFFT
    inner = (np.arange(128)[:, None] * lags[None, :]) % NFFT * turn
    base = np.concatenate([np.cos(inner), np.sin(inner)]).astype(np.float32)
    first = FIRST + 128 * np.arange(TILES, dtype=np.int64)
    outer = (first[:, None] * lags[None, :]) % NFFT * turn
    rot = np.zeros((TILES, 8, WIDE), np.float32)
    rot[:, 0] = np.cos(outer)
    rot[:, 1] = np.sin(outer)
    taper = np.sin(np.pi * (np.arange(BINS) + 0.5) / BINS) / math.sqrt(WINDOWS * BINS)
    rot[:, 2, :128] = taper.reshape(TILES, 128)
    return base, rot


def holder_of(t):
    return jnp.where(t < SPARE, 2 * t + lax.rem(t + lax.div(t, ROWS), 2), 1 + 10 * (t - SPARE))


def split(value):
    high = value.astype(BF16)
    return high, (value - high.astype(F32)).astype(BF16)


def kernel(
    spec_hbm, src_hbm, base_hbm, rot_hbm, out,
    spec, src, heard, mark, picked, items, chans, scales, base, rot, thi, tlo, mirror, cross, acc, part, parts,
    load_sem, hear_send, hear_recv, chip_send, chip_recv, item_send, item_recv, part_send, part_recv,
):
    r = lax.axis_index("recv")
    w = lax.axis_index("win")
    core = lax.rem(r, 2)
    first = r - core
    keeps = lax.div(w, WINDOWS // 2)
    regular = core == lax.rem(lax.div(r, 2) + lax.div(r, 2 * ROWS), 2)
    holder = regular | (r == 1) | (r == 11) | (r == 21)
    mine = jnp.where(regular, lax.div(r, 2), SPARE + lax.div(r, 10))
    own = core == keeps

    loads = [
        pltpu.make_async_copy(spec_hbm.at[0], spec.at[core], load_sem.at[0]),
        pltpu.make_async_copy(src_hbm, src, load_sem.at[1]),
        pltpu.make_async_copy(base_hbm, base, load_sem.at[2]),
        pltpu.make_async_copy(rot_hbm, rot, load_sem.at[3]),
    ]
    for load in loads:
        load.start()

    barrier = pltpu.get_barrier_semaphore()

    def greet(r2, w2):
        pl.semaphore_signal(barrier, inc=1, device_id=(r2, w2), device_id_type=MESH)

    greet(first + 1 - core, w)
    for d in range(1, WINDOWS):
        greet(first + keeps, lax.rem(w + d, WINDOWS))

    @pl.when(jnp.logical_not(own))
    def _():
        greet(first + keeps, w)

    @pl.when(holder)
    def _():
        def one(i, carry):
            greet(lax.rem(r + i, RECV), w)
            return carry

        lax.fori_loop(1, RECV, one, 0)

    pl.semaphore_wait(barrier, ITEMS - holder.astype(jnp.int32) + WINDOWS - own.astype(jnp.int32) + 1)

    def tell(i, carry):
        t = lax.div(i, FIRST_PART) * FIRST_PART + lax.rem(i + r, FIRST_PART)
        piece = spec_hbm.at[0, :, :, pl.ds(pl.multiple_of(t * 128, 128), 128)]

        r2 = holder_of(t)

        @pl.when(r2 == r)
        def _():
            pltpu.make_async_copy(piece, heard.at[r], hear_recv).start()

        @pl.when(r2 != r)
        def _():
            pltpu.make_async_remote_copy(
                piece, heard.at[r], hear_send, hear_recv, device_id=(r2, w), device_id_type=MESH
            ).start()

        return carry

    lax.fori_loop(0, TILES, tell, 0)
    chip = pltpu.make_async_remote_copy(
        spec_hbm.at[0], spec.at[core], chip_send, chip_recv, device_id=(first + 1 - core, w), device_id_type=MESH
    )
    chip.start()

    def shape(cc, c):
        both = spec[cc, c]
        power = jnp.sum(both * both, axis=(0, 1), keepdims=True) / BINS
        scale = jnp.broadcast_to(lax.rsqrt(power + 1e-06), (2, 128))
        for half in range(2):
            scales[cc, CHAN * half + c : CHAN * half + c + 1, :] = scale[0:1]
        for t in range(TILES):
            chans[cc, t, c : c + 1, :] = both[0:1, 128 * t : 128 * t + 128]
            chans[cc, t, CHAN + c : CHAN + c + 1, :] = both[1:2, 128 * t : 128 * t + 128]
        return scale

    loads[0].wait()
    for c in range(CHAN):
        mark[c] = shape(core, c)

    @pl.when(r == MARKER)
    def _():
        pltpu.make_async_copy(mark, heard.at[r], hear_recv).start()

    @pl.when(r != MARKER)
    def _():
        pltpu.make_async_remote_copy(
            mark, heard.at[r], hear_send, hear_recv, device_id=(MARKER, w), device_id_type=MESH
        ).start()

    loads[2].wait()
    loads[3].wait()

    def table(i, carry):
        u = lax.div(i, 8)
        row = pl.multiple_of(lax.rem(i, 8) * 16, 16)
        ct = rot[u, 0:1, :]
        st = rot[u, 1:2, :]
        cb = base[pl.ds(row, 16), :]
        sb = base[pl.ds(row + 128, 16), :]
        place = pl.ds(pl.multiple_of(u * 128 + row, 16), 16)
        thi[0, place, :], tlo[0, place, :] = split(cb * ct - sb * st)
        thi[1, place, :], tlo[1, place, :] = split(sb * ct + cb * st)
        return carry

    lax.fori_loop(0, TILES * 8, table, 0)

    loads[1].wait()

    @pl.when(holder)
    def _():
        pltpu.make_async_copy(heard, heard, hear_recv).wait()
        for k in range(NSRC):
            s = src[k]
            pair = heard[lax.shift_right_logical(s, 2), lax.bitwise_and(s, 3)]
            picked[k // PART, k % PART : k % PART + 1, :] = pair[0:1]
            picked[k // PART, PART + k % PART : PART + k % PART + 1, :] = pair[1:2]
        pltpu.make_async_copy(picked.at[core], items.at[mine], item_recv.at[mine]).start()

        def spread(i, carry):
            r2 = lax.div(i, 8) * 8 + lax.rem(r + i, 8)

            @pl.when(r2 != r)
            def _():
                pltpu.make_async_remote_copy(
                    picked.at[lax.rem(r2, 2)], items.at[mine], item_send, item_recv.at[mine], device_id=(r2, w), device_id_type=MESH
                ).start()

            return carry

        lax.fori_loop(0, RECV, spread, 0)

    chip.wait()
    for c in range(CHAN):
        shape(1 - core, c)

    def mirrored(i, carry):
        row = pl.multiple_of(i * 16, 16)
        m = lax.broadcasted_iota(jnp.int32, (16, WIDE), 0) + row
        j = lax.broadcasted_iota(jnp.int32, (16, WIDE), 1)
        mirror[pl.ds(row, 16), :] = jnp.where((m + j == HALF) & (m > 0), 1.0, 0.0).astype(BF16)
        return carry

    lax.fori_loop(0, WIDE // 16, mirrored, 0)

    upper = lax.broadcasted_iota(jnp.int32, (8, 128), 0) < CHAN

    def tile(t, carry):
        taper = rot[t, 2:3, 0:128]
        col = pl.ds(pl.multiple_of(t * 128, 128), 128)
        for cc in range(2):
            chan = chans[cc, t] * taper
            turned = pltpu.roll(chan, CHAN, 0)
            plus = jnp.where(upper, chan, -chan)
            pair = [
                items[t, k : k + 1, :] * plus + items[t, PART + k : PART + k + 1, :] * turned for k in range(PART)
            ]
            for p in range(2):
                re, im = [], []
                for g in (2 * p, 2 * p + 1):
                    a, b = pair[2 * g], pair[2 * g + 1]
                    re.append(jnp.where(upper, a, pltpu.roll(b, CHAN, 0)))
                    im.append(jnp.where(upper, pltpu.roll(a, CHAN, 0), b))
                at = 32 * cc + 16 * p
                for j, value in enumerate((re, im)):
                    high, low = split(jnp.concatenate(value, axis=0))
                    cross[j, at : at + 16, col] = high
                    cross[j, 64 + at : 64 + at + 16, col] = low
        return carry

    def arrived(t):
        pltpu.make_async_copy(items.at[t], items.at[t], item_recv.at[t]).wait()

    for start in range(0, TILES, GROUP):
        stop = min(start + GROUP, TILES)
        for t in range(start, stop):
            arrived(t)
        lax.fori_loop(start, stop, tile, 0)
        if stop == TILES:
            arrived(TILES)
        bins = slice(128 * start, 128 * stop)
        for n in range(4):
            j, cols = n // 2, slice(CUT * (n % 2), CUT * (n % 2) + CUT)
            both = jnp.dot(cross[j, :, bins], thi[j, bins, cols], preferred_element_type=F32)
            low = jnp.dot(cross[j, 0:64, bins], tlo[j, bins, cols], preferred_element_type=F32)
            value = both[0:64] + both[64:128] + low
            if start > 0:
                value = value + acc[n]
            if stop < TILES:
                acc[n] = value
                continue
            for g in range(8):
                cc, pair = g // 4, g % 4
                one = items[TILES, 2 * pair : 2 * pair + 1, :]
                two = items[TILES, 2 * pair + 1 : 2 * pair + 2, :]
                scale = jnp.where(upper, one, two) * scales[cc]
                part[n * 8 + g] = value[8 * g : 8 * g + 8] * jnp.concatenate([scale, scale], axis=1)
            for g in range(8):
                r2, w2 = first + g // 4, core * 4 + g % 4
                self = (r2 == r) & (w2 == w)

                @pl.when(self)
                def _(n=n, g=g):
                    pltpu.make_async_copy(part.at[n * 8 + g], parts.at[w, n], part_recv).start()

                @pl.when(jnp.logical_not(self))
                def _(n=n, g=g, r2=r2, w2=w2):
                    pltpu.make_async_remote_copy(
                        part.at[n * 8 + g], parts.at[w, n], part_send, part_recv, device_id=(r2, w2), device_id_type=MESH
                    ).start()

    pltpu.make_async_copy(parts, parts, part_recv).wait()
    total = []
    for n in range(4):
        value = parts[0, n]
        for v in range(1, WINDOWS):
            value = value + parts[v, n]
        total.append(value)
    even = jnp.concatenate(total[0:2], axis=1)
    odd = jnp.concatenate(total[2:4], axis=1)
    before = even + odd
    one = before.astype(BF16)
    rest = before - one.astype(F32)
    two = rest.astype(BF16)
    three = (rest - two.astype(F32)).astype(BF16)
    thrice = jnp.dot(jnp.concatenate([one, two, three], axis=0), mirror[...], preferred_element_type=F32)
    before = thrice[0:8] + thrice[8:16] + thrice[16:24]
    after = pltpu.roll(even - odd, HALF, 1)
    lane = lax.broadcasted_iota(jnp.int32, (8, WIDE), 1)
    left = jnp.where(lane < HALF, before, after)
    for k in range(2):
        out[k, :, 0:WIDE] = left[CHAN * k : CHAN * k + CHAN]
        out[k, :, WIDE:LAGS] = after[CHAN * k : CHAN * k + CHAN, 0 : LAGS - WIDE]

    @pl.when(holder)
    def _():
        pltpu.make_async_copy(heard.at[pl.ds(0, ITEMS - 1)], heard.at[pl.ds(0, ITEMS - 1)], hear_send).wait()
        pltpu.make_async_copy(items.at[pl.ds(0, RECV - 1)], items.at[pl.ds(0, RECV - 1)], item_send).wait()

    @pl.when(jnp.logical_not(holder))
    def _():
        pltpu.make_async_copy(heard.at[pl.ds(0, ITEMS)], heard.at[pl.ds(0, ITEMS)], hear_send).wait()

    @pl.when(own)
    def _():
        pltpu.make_async_copy(part.at[pl.ds(0, 28)], part.at[pl.ds(0, 28)], part_send).wait()

    @pl.when(jnp.logical_not(own))
    def _():
        pltpu.make_async_copy(part, part, part_send).wait()


def shards(spectra, sources):
    base, rot = tables()
    anywhere = pl.BlockSpec(memory_space=pl.ANY)
    vmem = pltpu.VMEM
    dma = pltpu.SemaphoreType.DMA
    return pl.pallas_call(
        kernel,
        out_shape=jax.ShapeDtypeStruct((NSRC // WINDOWS, CHAN, LAGS), F32),
        in_specs=[anywhere] * 4,
        out_specs=pl.BlockSpec(memory_space=vmem),
        scratch_shapes=[
            vmem((2, CHAN, 2, BINS), F32),
            pltpu.SMEM((NSRC,), jnp.int32),
            vmem((RECV, CHAN, 2, 128), F32),
            vmem((CHAN, 2, 128), F32),
            vmem((2, 2 * PART, 128), F32),
            vmem((RECV, 2 * PART, 128), F32),
            vmem((2, TILES, 8, 128), F32),
            vmem((2, 8, 128), F32),
            vmem((256, WIDE), F32),
            vmem((TILES, 8, WIDE), F32),
            vmem((2, BINS, WIDE), BF16),
            vmem((2, BINS, WIDE), BF16),
            vmem((WIDE, WIDE), BF16),
            vmem((2, 128, BINS), BF16),
            vmem((4, 64, CUT), F32),
            vmem((32, 8, CUT), F32),
            vmem((WINDOWS, 4, 8, CUT), F32),
            dma((4,)),
            dma,
            dma,
            dma,
            dma,
            dma,
            dma((ITEMS,)),
            dma,
            dma,
        ],
        compiler_params=pltpu.CompilerParams(
            collective_id=0, has_side_effects=True, vmem_limit_bytes=60 * 1024 * 1024
        ),
    )(spectra, sources, jnp.asarray(base), jnp.asarray(rot))


def solution(mesh):
    in_specs = (P("win", "recv", None, None), P())
    out_specs = P("win", "recv", None)
    return jax.shard_map(shards, mesh=mesh, in_specs=in_specs, out_specs=out_specs, check_vma=False)
```

time: 819 us -> 45.1 us (0.06)
  waiting for transfers between devices: 638 us -> 0 us
  matrix products: 155 us -> 0 us
  Pallas kernels: 0 us -> 43.5 us
  between operations: 14.2 us -> 0.01 us
    psum x1 -> x0, waiting for transfers between devices: 522 us -> none  [shards(): source = lax.psum(local, 'recv').reshape(nsrc, 2, nbins)]
    dot_general x35 -> x0, matrix products: 155 us -> none  [the longest x17 77.7 us: step(): return total + jnp.dot(right, sines, precision=lax.Precision.HIGHEST)]
    unnamed x3 -> x0, waiting for transfers between devices: 115 us -> none
    pallas_call x0 -> x1, Pallas kernels: none -> 43.5 us  [shards(): pl.pallas_call(kernel, out_shape=jax.ShapeDtypeStruct((NSRC // WINDOWS, C...]
  transfers between devices with their start and end apart: 2 -> 0, of which waited for: 2 -> 0; matrix products, arithmetic and copies ran while one was open for 0% -> 0% of each run, Pallas kernels for 0% -> 0%
where the time goes in v2:
time: 45.1 us; the launch traced here: 44.9 us
  Pallas kernels  43.5 us (96%)
  local copies, waits for them, and re-layouts  1.38 us (3%)
    pallas_call x1, Pallas kernels, shards(): pl.pallas_call(kernel, out_shape=jax.ShapeDtypeStruct((NSRC // WINDOWS, C...  43.5 us
    unnamed x1, local copies, waits for them, and re-layouts  1.38 us

profile of v2, /device:TPU:1, one launch (start us, length us, event | category | flops | bytes accessed | tf_op | source)
XLA Modules:
  0.0 44.9 jit_solution(7621208995202035260)
XLA Ops:
  0.0 43.5 %shard_map.46 = f32[2,4,1001]{2,1,0:T(4,128)} custom-call(f32[1,4,2,4352]{3,2,1,0:T(2,128)} %spec_hbm.1, s32[16]{0:T(128)} %src_hbm.1, f32[256,512]{1,0:T(8,128)} %constant.4.clone.base_hbm, f32[34,8,512]{2,1,0:T(8,128)} %constant.5.clone.rot_hbm), custom_call_target="tpu_custom_call" | custom-call | tf_op jit(solution)/shard_map/pallas_call | solution.py:322
  43.5 1.4 %copy.6 = f32[2,4,1001]{2,1,0:T(4,128)} copy(f32[2,4,1001]{2,1,0:T(4,128)} %shard_map.46) | data formatting | bytes 64064

commit v3 on v2

--- a/solution.py
+++ b/solution.py
@@ -23,9 +23,12 @@
 PART = NSRC // 2
 WIDE = 512
 CUT = 256
-GROUP = 17
+GROUPS = ((0, 12), (12, 20), (20, 28), (28, 34))
 FIRST_PART = 17
-MARKER = 21
+MARKER = 34
+URGENT_Z = (0, 1, 2, 3, 3.5, 4.5, 5.5, 6)
+URGENT_Y = (-0.9, -0.3, 0.4, 0)
+ORDER = sorted(range(RECV), key=lambda r2: URGENT_Z[r2 // 8] + URGENT_Y[r2 // 2 % 4])
 SPARE = RECV // 2
 MESH = pl.DeviceIdType.MESH
 F32 = jnp.float32
@@ -48,7 +51,7 @@
 
 
 def holder_of(t):
-    return jnp.where(t < SPARE, 2 * t + lax.rem(t + lax.div(t, ROWS), 2), 1 + 10 * (t - SPARE))
+    return t
 
 
 def split(value):
@@ -66,9 +69,8 @@
     core = lax.rem(r, 2)
     first = r - core
     keeps = lax.div(w, WINDOWS // 2)
-    regular = core == lax.rem(lax.div(r, 2) + lax.div(r, 2 * ROWS), 2)
-    holder = regular | (r == 1) | (r == 11) | (r == 21)
-    mine = jnp.where(regular, lax.div(r, 2), SPARE + lax.div(r, 10))
+    holder = r < ITEMS
+    mine = r
     own = core == keeps
 
     loads = [
@@ -85,47 +87,22 @@
     def greet(r2, w2):
         pl.semaphore_signal(barrier, inc=1, device_id=(r2, w2), device_id_type=MESH)
 
+    @pl.when(holder)
+    def _():
+        def one(i, carry):
+            step = i + RECV // 2
+            greet(lax.bitwise_and(r + jnp.where(step < RECV, step, step - RECV + 1), RECV - 1), w)
+            return carry
+
+        lax.fori_loop(0, RECV - 1, one, 0)
+
     greet(first + 1 - core, w)
     for d in range(1, WINDOWS):
-        greet(first + keeps, lax.rem(w + d, WINDOWS))
+        greet(first + keeps, lax.bitwise_and(w + d, WINDOWS - 1))
 
     @pl.when(jnp.logical_not(own))
     def _():
         greet(first + keeps, w)
-
-    @pl.when(holder)
-    def _():
-        def one(i, carry):
-            greet(lax.rem(r + i, RECV), w)
-            return carry
-
-        lax.fori_loop(1, RECV, one, 0)
-
-    pl.semaphore_wait(barrier, ITEMS - holder.astype(jnp.int32) + WINDOWS - own.astype(jnp.int32) + 1)
-
-    def tell(i, carry):
-        t = lax.div(i, FIRST_PART) * FIRST_PART + lax.rem(i + r, FIRST_PART)
-        piece = spec_hbm.at[0, :, :, pl.ds(pl.multiple_of(t * 128, 128), 128)]
-
-        r2 = holder_of(t)
-
-        @pl.when(r2 == r)
-        def _():
-            pltpu.make_async_copy(piece, heard.at[r], hear_recv).start()
-
-        @pl.when(r2 != r)
-        def _():
-            pltpu.make_async_remote_copy(
-                piece, heard.at[r], hear_send, hear_recv, device_id=(r2, w), device_id_type=MESH
-            ).start()
-
-        return carry
-
-    lax.fori_loop(0, TILES, tell, 0)
-    chip = pltpu.make_async_remote_copy(
-        spec_hbm.at[0], spec.at[core], chip_send, chip_recv, device_id=(first + 1 - core, w), device_id_type=MESH
-    )
-    chip.start()
 
     def shape(cc, c):
         both = spec[cc, c]
@@ -142,6 +119,35 @@
     for c in range(CHAN):
         mark[c] = shape(core, c)
 
+    pl.semaphore_wait(barrier, ITEMS - holder.astype(jnp.int32) + WINDOWS - own.astype(jnp.int32) + 1)
+
+    def tell(i, carry):
+        t = turn + lax.rem(i, FIRST_PART)
+        t = jnp.where(t < FIRST_PART, t, t - FIRST_PART) + lax.div(i, FIRST_PART) * FIRST_PART
+        piece = spec.at[core, :, :, pl.ds(pl.multiple_of(t * 128, 128), 128)]
+
+        r2 = holder_of(t)
+
+        @pl.when(r2 == r)
+        def _():
+            pltpu.make_async_copy(piece, heard.at[r], hear_recv).start()
+
+        @pl.when(r2 != r)
+        def _():
+            pltpu.make_async_remote_copy(
+                piece, heard.at[r], hear_send, hear_recv, device_id=(r2, w), device_id_type=MESH
+            ).start()
+
+        return carry
+
+    turn = lax.rem(r, FIRST_PART)
+    for i in range(TILES):
+        tell(i, 0)
+    chip = pltpu.make_async_remote_copy(
+        spec_hbm.at[0], spec.at[core], chip_send, chip_recv, device_id=(first + 1 - core, w), device_id_type=MESH
+    )
+    chip.start()
+
     @pl.when(r == MARKER)
     def _():
         pltpu.make_async_copy(mark, heard.at[r], hear_recv).start()
@@ -155,14 +161,21 @@
     loads[2].wait()
     loads[3].wait()
 
+    z = lax.shift_right_logical(r, 3)
+
+    def tile_at(p):
+        near = p
+        return jnp.where(p < SPARE, near, p)
+
     def table(i, carry):
-        u = lax.div(i, 8)
-        row = pl.multiple_of(lax.rem(i, 8) * 16, 16)
+        p = lax.shift_right_logical(i, 3)
+        u = tile_at(p)
+        row = pl.multiple_of(lax.bitwise_and(i, 7) * 16, 16)
         ct = rot[u, 0:1, :]
         st = rot[u, 1:2, :]
         cb = base[pl.ds(row, 16), :]
         sb = base[pl.ds(row + 128, 16), :]
-        place = pl.ds(pl.multiple_of(u * 128 + row, 16), 16)
+        place = pl.ds(pl.multiple_of(p * 128 + row, 16), 16)
         thi[0, place, :], tlo[0, place, :] = split(cb * ct - sb * st)
         thi[1, place, :], tlo[1, place, :] = split(sb * ct + cb * st)
         return carry
@@ -182,17 +195,18 @@
         pltpu.make_async_copy(picked.at[core], items.at[mine], item_recv.at[mine]).start()
 
         def spread(i, carry):
-            r2 = lax.div(i, 8) * 8 + lax.rem(r + i, 8)
+            r2 = i
 
             @pl.when(r2 != r)
             def _():
                 pltpu.make_async_remote_copy(
-                    picked.at[lax.rem(r2, 2)], items.at[mine], item_send, item_recv.at[mine], device_id=(r2, w), device_id_type=MESH
+                    picked.at[i % 2], items.at[mine], item_send, item_recv.at[mine], device_id=(r2, w), device_id_type=MESH
                 ).start()
 
             return carry
 
-        lax.fori_loop(0, RECV, spread, 0)
+        for i in ORDER:
+            spread(i, 0)
 
     chip.wait()
     for c in range(CHAN):
@@ -207,11 +221,14 @@
 
     lax.fori_loop(0, WIDE // 16, mirrored, 0)
 
+    x = lax.shift_right_logical(w, 1)
+    ahead = jnp.where((lax.bitwise_and(2 * core + 1 - x + 4, 3) == 2) | (2 * core == x), 2, 0)
     upper = lax.broadcasted_iota(jnp.int32, (8, 128), 0) < CHAN
 
-    def tile(t, carry):
+    def tile(p, carry):
+        t = tile_at(p)
         taper = rot[t, 2:3, 0:128]
-        col = pl.ds(pl.multiple_of(t * 128, 128), 128)
+        col = pl.ds(pl.multiple_of(p * 128, 128), 128)
         for cc in range(2):
             chan = chans[cc, t] * taper
             turned = pltpu.roll(chan, CHAN, 0)
@@ -219,13 +236,13 @@
             pair = [
                 items[t, k : k + 1, :] * plus + items[t, PART + k : PART + k + 1, :] * turned for k in range(PART)
             ]
-            for p in range(2):
+            for h in range(2):
                 re, im = [], []
-                for g in (2 * p, 2 * p + 1):
+                for g in (2 * h, 2 * h + 1):
                     a, b = pair[2 * g], pair[2 * g + 1]
                     re.append(jnp.where(upper, a, pltpu.roll(b, CHAN, 0)))
                     im.append(jnp.where(upper, pltpu.roll(a, CHAN, 0), b))
-                at = 32 * cc + 16 * p
+                at = 32 * cc + 16 * h
                 for j, value in enumerate((re, im)):
                     high, low = split(jnp.concatenate(value, axis=0))
                     cross[j, at : at + 16, col] = high
@@ -235,10 +252,9 @@
     def arrived(t):
         pltpu.make_async_copy(items.at[t], items.at[t], item_recv.at[t]).wait()
 
-    for start in range(0, TILES, GROUP):
-        stop = min(start + GROUP, TILES)
-        for t in range(start, stop):
-            arrived(t)
+    for start, stop in GROUPS:
+        for p in range(start, stop):
+            arrived(tile_at(p))
         lax.fori_loop(start, stop, tile, 0)
         if stop == TILES:
             arrived(TILES)
@@ -260,25 +276,27 @@
                 scale = jnp.where(upper, one, two) * scales[cc]
                 part[n * 8 + g] = value[8 * g : 8 * g + 8] * jnp.concatenate([scale, scale], axis=1)
             for g in range(8):
-                r2, w2 = first + g // 4, core * 4 + g % 4
+                pair = lax.bitwise_xor(g // 2, ahead)
+                r2, w2 = first + g % 2, core * 4 + pair
+                g = n * 8 + (g % 2) * 4 + pair
                 self = (r2 == r) & (w2 == w)
 
                 @pl.when(self)
                 def _(n=n, g=g):
-                    pltpu.make_async_copy(part.at[n * 8 + g], parts.at[w, n], part_recv).start()
+                    pltpu.make_async_copy(part.at[g], parts.at[n, w], part_recv.at[n]).start()
 
                 @pl.when(jnp.logical_not(self))
                 def _(n=n, g=g, r2=r2, w2=w2):
                     pltpu.make_async_remote_copy(
-                        part.at[n * 8 + g], parts.at[w, n], part_send, part_recv, device_id=(r2, w2), device_id_type=MESH
+                        part.at[g], parts.at[n, w], part_send, part_recv.at[n], device_id=(r2, w2), device_id_type=MESH
                     ).start()
 
-    pltpu.make_async_copy(parts, parts, part_recv).wait()
     total = []
     for n in range(4):
-        value = parts[0, n]
+        pltpu.make_async_copy(parts.at[n], parts.at[n], part_recv.at[n]).wait()
+        value = parts[n, 0]
         for v in range(1, WINDOWS):
-            value = value + parts[v, n]
+            value = value + parts[n, v]
         total.append(value)
     even = jnp.concatenate(total[0:2], axis=1)
     odd = jnp.concatenate(total[2:4], axis=1)
@@ -321,7 +339,7 @@
     dma = pltpu.SemaphoreType.DMA
     return pl.pallas_call(
         kernel,
-        out_shape=jax.ShapeDtypeStruct((NSRC // WINDOWS, CHAN, LAGS), F32),
+        out_shape=pltpu.VMEM((NSRC // WINDOWS, CHAN, LAGS), F32),
         in_specs=[anywhere] * 4,
         out_specs=pl.BlockSpec(memory_space=vmem),
         scratch_shapes=[
@@ -341,7 +359,7 @@
             vmem((2, 128, BINS), BF16),
             vmem((4, 64, CUT), F32),
             vmem((32, 8, CUT), F32),
-            vmem((WINDOWS, 4, 8, CUT), F32),
+            vmem((4, WINDOWS, 8, CUT), F32),
             dma((4,)),
             dma,
             dma,
@@ -350,7 +368,7 @@
             dma,
             dma((ITEMS,)),
             dma,
-            dma,
+            dma((4,)),
         ],
         compiler_params=pltpu.CompilerParams(
             collective_id=0, has_side_effects=True, vmem_limit_bytes=60 * 1024 * 1024

time: 45.1 us -> 43.3 us (0.960)
  the two profiles are of different devices: /device:TPU:1 before, /device:TPU:321 now
where the time goes in v3:
time: 43.3 us; the launch traced here: 43.2 us
  Pallas kernels  42.6 us (98%)
  local copies, waits for them, and re-layouts  0.62 us (1%)
    pallas_call x1, Pallas kernels, shards(): pl.pallas_call(kernel, out_shape=pltpu.VMEM((NSRC // WINDOWS, CHAN, LAGS)...  42.6 us

profile of v3, /device:TPU:321, one launch (start us, length us, event | category | flops | bytes accessed | tf_op | source)
XLA Modules:
  0.0 43.2 jit_solution(12273754232702089834)
XLA Ops:
  0.0 42.6 %shard_map.46 = f32[2,4,1001]{2,1,0:T(4,128)S(1)} custom-call(f32[1,4,2,4352]{3,2,1,0:T(2,128)} %spec_hbm.1, s32[16]{0:T(128)} %src_hbm.1, f32[256,512]{1,0:T(8,128)} %constant.4.clone.base_hbm, f32[34,8,512]{2,1,0:T(8,128)} %constant.5.clone.rot_hbm), custom_call_target="tpu_custom_call" | custom-call | tf_op jit(solution)/shard_map/pallas_call | solution.py:340
  42.6 0.6 %copy.6 = f32[2,4,1001]{2,1,0:T(4,128)} copy(f32[2,4,1001]{2,1,0:T(4,128)S(1)} %shard_map.46) | data formatting | bytes 64064

commit v4 on v3

--- a/solution.py
+++ b/solution.py
@@ -20,14 +20,15 @@
 RECV = 64
 TILES = BINS // 128
 ITEMS = TILES + 1
-PART = NSRC // 2
+TEAM = 4
+PART = NSRC // TEAM
 WIDE = 512
 CUT = 256
 GROUPS = ((0, 12), (12, 20), (20, 28), (28, 34))
 FIRST_PART = 17
 MARKER = 34
-URGENT_Z = (0, 1, 2, 3, 3.5, 4.5, 5.5, 6)
-URGENT_Y = (-0.9, -0.3, 0.4, 0)
+URGENT_Z = (0, 0.3, 2, 2.3, 4, 4.3, 5, 5.3)
+URGENT_Y = (-0.2, -0.1, 0.1, 0)
 ORDER = sorted(range(RECV), key=lambda r2: URGENT_Z[r2 // 8] + URGENT_Y[r2 // 2 % 4])
 SPARE = RECV // 2
 MESH = pl.DeviceIdType.MESH
@@ -50,8 +51,8 @@
     return base, rot
 
 
-def holder_of(t):
-    return t
+def member_of(r):
+    return (r & 1) * 2 + ((r >> 3) & 1)
 
 
 def split(value):
@@ -62,19 +63,25 @@
 def kernel(
     spec_hbm, src_hbm, base_hbm, rot_hbm, out,
     spec, src, heard, mark, picked, items, chans, scales, base, rot, thi, tlo, mirror, cross, acc, part, parts,
-    load_sem, hear_send, hear_recv, chip_send, chip_recv, item_send, item_recv, part_send, part_recv,
+    load_sem, hear_send, hear_recv, share_send, share_recv, item_send, item_recv, part_send, part_recv,
 ):
     r = lax.axis_index("recv")
     w = lax.axis_index("win")
     core = lax.rem(r, 2)
-    first = r - core
-    keeps = lax.div(w, WINDOWS // 2)
+    me = member_of(r)
+    team = r - core - 8 * (me & 1)
+
+    def member(q):
+        return team + 8 * (q & 1) + (q >> 1)
+
+    keeps = jnp.where(w < TEAM, w, WINDOWS - 1 - w)
     holder = r < ITEMS
-    mine = r
-    own = core == keeps
+    own = me == keeps
+    other_core = r + 1 - 2 * core
+    other_chip = member(me ^ 1)
 
     loads = [
-        pltpu.make_async_copy(spec_hbm.at[0], spec.at[core], load_sem.at[0]),
+        pltpu.make_async_copy(spec_hbm.at[0], spec.at[me], load_sem.at[0]),
         pltpu.make_async_copy(src_hbm, src, load_sem.at[1]),
         pltpu.make_async_copy(base_hbm, base, load_sem.at[2]),
         pltpu.make_async_copy(rot_hbm, rot, load_sem.at[3]),
@@ -96,13 +103,14 @@
 
         lax.fori_loop(0, RECV - 1, one, 0)
 
-    greet(first + 1 - core, w)
+    greet(other_core, w)
+    greet(other_chip, w)
     for d in range(1, WINDOWS):
-        greet(first + keeps, lax.bitwise_and(w + d, WINDOWS - 1))
+        greet(member(keeps), lax.bitwise_and(w + d, WINDOWS - 1))
 
     @pl.when(jnp.logical_not(own))
     def _():
-        greet(first + keeps, w)
+        greet(member(keeps), w)
 
     def shape(cc, c):
         both = spec[cc, c]
@@ -117,25 +125,23 @@
 
     loads[0].wait()
     for c in range(CHAN):
-        mark[c] = shape(core, c)
-
-    pl.semaphore_wait(barrier, ITEMS - holder.astype(jnp.int32) + WINDOWS - own.astype(jnp.int32) + 1)
+        mark[c] = shape(me, c)
+
+    pl.semaphore_wait(barrier, ITEMS - holder.astype(jnp.int32) + WINDOWS - own.astype(jnp.int32) + 2)
 
     def tell(i, carry):
         t = turn + lax.rem(i, FIRST_PART)
         t = jnp.where(t < FIRST_PART, t, t - FIRST_PART) + lax.div(i, FIRST_PART) * FIRST_PART
-        piece = spec.at[core, :, :, pl.ds(pl.multiple_of(t * 128, 128), 128)]
-
-        r2 = holder_of(t)
-
-        @pl.when(r2 == r)
+        piece = spec.at[me, :, :, pl.ds(pl.multiple_of(t * 128, 128), 128)]
+
+        @pl.when(t == r)
         def _():
             pltpu.make_async_copy(piece, heard.at[r], hear_recv).start()
 
-        @pl.when(r2 != r)
+        @pl.when(t != r)
         def _():
             pltpu.make_async_remote_copy(
-                piece, heard.at[r], hear_send, hear_recv, device_id=(r2, w), device_id_type=MESH
+                piece, heard.at[r], hear_send, hear_recv, device_id=(t, w), device_id_type=MESH
             ).start()
 
         return carry
@@ -143,10 +149,17 @@
     turn = lax.rem(r, FIRST_PART)
     for i in range(TILES):
         tell(i, 0)
-    chip = pltpu.make_async_remote_copy(
-        spec_hbm.at[0], spec.at[core], chip_send, chip_recv, device_id=(first + 1 - core, w), device_id_type=MESH
-    )
-    chip.start()
+
+    def share(q, r2, sem):
+        return pltpu.make_async_remote_copy(
+            spec.at[q], spec.at[q], share_send.at[sem], share_recv.at[sem], device_id=(r2, w), device_id_type=MESH
+        )
+
+    to_chip = share(me, other_chip, 0)
+    to_core = share(me, other_core, 1)
+    to_core_too = share(me ^ 1, other_core, 2)
+    to_chip.start()
+    to_core.start()
 
     @pl.when(r == MARKER)
     def _():
@@ -162,10 +175,10 @@
     loads[3].wait()
 
     z = lax.shift_right_logical(r, 3)
+    flip = jnp.where((z >= 2) & (z <= 5), 24, 0)
 
     def tile_at(p):
-        near = p
-        return jnp.where(p < SPARE, near, p)
+        return jnp.where(p < SPARE, p ^ flip, p)
 
     def table(i, carry):
         p = lax.shift_right_logical(i, 3)
@@ -190,9 +203,11 @@
         for k in range(NSRC):
             s = src[k]
             pair = heard[lax.shift_right_logical(s, 2), lax.bitwise_and(s, 3)]
-            picked[k // PART, k % PART : k % PART + 1, :] = pair[0:1]
-            picked[k // PART, PART + k % PART : PART + k % PART + 1, :] = pair[1:2]
-        pltpu.make_async_copy(picked.at[core], items.at[mine], item_recv.at[mine]).start()
+            v = k // 2
+            q, place = min(v, WINDOWS - 1 - v), 2 * (v // TEAM) + k % 2
+            picked[q, place : place + 1, :] = pair[0:1]
+            picked[q, PART + place : PART + place + 1, :] = pair[1:2]
+        pltpu.make_async_copy(picked.at[me], items.at[r], item_recv.at[r]).start()
 
         def spread(i, carry):
             r2 = i
@@ -200,7 +215,7 @@
             @pl.when(r2 != r)
             def _():
                 pltpu.make_async_remote_copy(
-                    picked.at[i % 2], items.at[mine], item_send, item_recv.at[mine], device_id=(r2, w), device_id_type=MESH
+                    picked.at[member_of(i)], items.at[r], item_send, item_recv.at[r], device_id=(r2, w), device_id_type=MESH
                 ).start()
 
             return carry
@@ -208,9 +223,16 @@
         for i in ORDER:
             spread(i, 0)
 
-    chip.wait()
+    to_chip.wait()
+    to_core_too.start()
     for c in range(CHAN):
-        shape(1 - core, c)
+        shape(me ^ 1, c)
+    to_core.wait()
+    for c in range(CHAN):
+        shape(me ^ 2, c)
+    to_core_too.wait()
+    for c in range(CHAN):
+        shape(me ^ 3, c)
 
     def mirrored(i, carry):
         row = pl.multiple_of(i * 16, 16)
@@ -221,32 +243,32 @@
 
     lax.fori_loop(0, WIDE // 16, mirrored, 0)
 
-    x = lax.shift_right_logical(w, 1)
-    ahead = jnp.where((lax.bitwise_and(2 * core + 1 - x + 4, 3) == 2) | (2 * core == x), 2, 0)
+    x = w >> 1
+    near_x = ((me >> 1) - x) & 3
+    far_x = (3 - (me >> 1) - x) & 3
+    ahead = ((far_x == 2) | (near_x == 0)).astype(jnp.int32)
     upper = lax.broadcasted_iota(jnp.int32, (8, 128), 0) < CHAN
 
     def tile(p, carry):
         t = tile_at(p)
         taper = rot[t, 2:3, 0:128]
         col = pl.ds(pl.multiple_of(p * 128, 128), 128)
-        for cc in range(2):
+        for cc in range(TEAM):
             chan = chans[cc, t] * taper
             turned = pltpu.roll(chan, CHAN, 0)
             plus = jnp.where(upper, chan, -chan)
             pair = [
                 items[t, k : k + 1, :] * plus + items[t, PART + k : PART + k + 1, :] * turned for k in range(PART)
             ]
-            for h in range(2):
-                re, im = [], []
-                for g in (2 * h, 2 * h + 1):
-                    a, b = pair[2 * g], pair[2 * g + 1]
-                    re.append(jnp.where(upper, a, pltpu.roll(b, CHAN, 0)))
-                    im.append(jnp.where(upper, pltpu.roll(a, CHAN, 0), b))
-                at = 32 * cc + 16 * h
-                for j, value in enumerate((re, im)):
-                    high, low = split(jnp.concatenate(value, axis=0))
-                    cross[j, at : at + 16, col] = high
-                    cross[j, 64 + at : 64 + at + 16, col] = low
+            re, im = [], []
+            for a, b in (pair[0:2], pair[2:4]):
+                re.append(jnp.where(upper, a, pltpu.roll(b, CHAN, 0)))
+                im.append(jnp.where(upper, pltpu.roll(a, CHAN, 0), b))
+            at = 16 * cc
+            for j, value in enumerate((re, im)):
+                high, low = split(jnp.concatenate(value, axis=0))
+                cross[j, at : at + 16, col] = high
+                cross[j, 64 + at : 64 + at + 16, col] = low
         return carry
 
     def arrived(t):
@@ -260,7 +282,7 @@
             arrived(TILES)
         bins = slice(128 * start, 128 * stop)
         for n in range(4):
-            j, cols = n // 2, slice(CUT * (n % 2), CUT * (n % 2) + CUT)
+            j, cols = n % 2, slice(CUT * (n // 2), CUT * (n // 2) + CUT)
             both = jnp.dot(cross[j, :, bins], thi[j, bins, cols], preferred_element_type=F32)
             low = jnp.dot(cross[j, 0:64, bins], tlo[j, bins, cols], preferred_element_type=F32)
             value = both[0:64] + both[64:128] + low
@@ -270,15 +292,14 @@
                 acc[n] = value
                 continue
             for g in range(8):
-                cc, pair = g // 4, g % 4
-                one = items[TILES, 2 * pair : 2 * pair + 1, :]
-                two = items[TILES, 2 * pair + 1 : 2 * pair + 2, :]
-                scale = jnp.where(upper, one, two) * scales[cc]
+                cc, j = g // 2, g % 2
+                scale = jnp.where(upper, items[TILES, 2 * j : 2 * j + 1, :], items[TILES, 2 * j + 1 : 2 * j + 2, :])
+                scale = scale * scales[cc]
                 part[n * 8 + g] = value[8 * g : 8 * g + 8] * jnp.concatenate([scale, scale], axis=1)
-            for g in range(8):
-                pair = lax.bitwise_xor(g // 2, ahead)
-                r2, w2 = first + g % 2, core * 4 + pair
-                g = n * 8 + (g % 2) * 4 + pair
+            for i in range(8):
+                cc, j = me ^ (1, 3, 2, 0)[i % 4], ahead ^ (i // 4)
+                r2, w2 = member(cc), jnp.where(j == 0, me, WINDOWS - 1 - me)
+                g = n * 8 + cc * 2 + j
                 self = (r2 == r) & (w2 == w)
 
                 @pl.when(self)
@@ -298,8 +319,8 @@
         for v in range(1, WINDOWS):
             value = value + parts[n, v]
         total.append(value)
-    even = jnp.concatenate(total[0:2], axis=1)
-    odd = jnp.concatenate(total[2:4], axis=1)
+    even = jnp.concatenate(total[0::2], axis=1)
+    odd = jnp.concatenate(total[1::2], axis=1)
     before = even + odd
     one = before.astype(BF16)
     rest = before - one.astype(F32)
@@ -343,14 +364,14 @@
         in_specs=[anywhere] * 4,
         out_specs=pl.BlockSpec(memory_space=vmem),
         scratch_shapes=[
-            vmem((2, CHAN, 2, BINS), F32),
+            vmem((TEAM, CHAN, 2, BINS), F32),
             pltpu.SMEM((NSRC,), jnp.int32),
             vmem((RECV, CHAN, 2, 128), F32),
             vmem((CHAN, 2, 128), F32),
-            vmem((2, 2 * PART, 128), F32),
+            vmem((TEAM, 2 * PART, 128), F32),
             vmem((RECV, 2 * PART, 128), F32),
-            vmem((2, TILES, 8, 128), F32),
-            vmem((2, 8, 128), F32),
+            vmem((TEAM, TILES, 8, 128), F32),
+            vmem((TEAM, 8, 128), F32),
             vmem((256, WIDE), F32),
             vmem((TILES, 8, WIDE), F32),
             vmem((2, BINS, WIDE), BF16),
@@ -363,8 +384,8 @@
             dma((4,)),
             dma,
             dma,
-            dma,
-            dma,
+            dma((3,)),
+            dma((3,)),
             dma,
             dma((ITEMS,)),
             dma,

time: 43.3 us -> 40 us (0.924)
  the two profiles are of different devices: /device:TPU:321 before, /device:TPU:1 now
where the time goes in v4:
time: 40 us; the launch traced here: 39.9 us
  Pallas kernels  39.3 us (98%)
  local copies, waits for them, and re-layouts  0.62 us (2%)
    pallas_call x1, Pallas kernels, shards(): pl.pallas_call(kernel, out_shape=pltpu.VMEM((NSRC // WINDOWS, CHAN, LAGS)...  39.3 us

profile of v4, /device:TPU:1, one launch (start us, length us, event | category | flops | bytes accessed | tf_op | source)
XLA Modules:
  0.0 39.9 jit_solution(10721854672091952763)
XLA Ops:
  0.0 39.3 %shard_map.46 = f32[2,4,1001]{2,1,0:T(4,128)S(1)} custom-call(f32[1,4,2,4352]{3,2,1,0:T(2,128)} %spec_hbm.1, s32[16]{0:T(128)} %src_hbm.1, f32[256,512]{1,0:T(8,128)} %constant.4.clone.base_hbm, f32[34,8,512]{2,1,0:T(8,128)} %constant.5.clone.rot_hbm), custom_call_target="tpu_custom_call" | custom-call | tf_op jit(solution)/shard_map/pallas_call | solution.py:361
  39.3 0.6 %copy.6 = f32[2,4,1001]{2,1,0:T(4,128)} copy(f32[2,4,1001]{2,1,0:T(4,128)S(1)} %shard_map.46) | data formatting | bytes 64064

commit v5 on v4

--- a/solution.py
+++ b/solution.py
@@ -25,8 +25,15 @@
 WIDE = 512
 CUT = 256
 GROUPS = ((0, 12), (12, 20), (20, 28), (28, 34))
-FIRST_PART = 17
-MARKER = 34
+NEAR = sorted(((z, y) for z in range(4) for y in range(4)), key=lambda at: at[0] + 2 * min(at[1], 4 - at[1]))
+NEAR_Z = [sum(NEAR[8 * h + i][0] << (2 * i) for i in range(8)) for h in range(2)]
+NEAR_Y = [sum(NEAR[8 * h + i][1] << (2 * i) for i in range(8)) for h in range(2)]
+FAR = sorted(
+    ((z, y, c) for z in range(8) for y in range(ROWS) for c in range(2) if z or y or c),
+    key=lambda at: -min(at[0], 8 - at[0]) - 2 * min(at[1], 4 - at[1]),
+)
+MARKER = 32
+LATE = 56
 URGENT_Z = (0, 0.3, 2, 2.3, 4, 4.3, 5, 5.3)
 URGENT_Y = (-0.2, -0.1, 0.1, 0)
 ORDER = sorted(range(RECV), key=lambda r2: URGENT_Z[r2 // 8] + URGENT_Y[r2 // 2 % 4])
@@ -62,7 +69,7 @@
 
 def kernel(
     spec_hbm, src_hbm, base_hbm, rot_hbm, out,
-    spec, src, heard, mark, picked, items, chans, scales, base, rot, thi, tlo, mirror, cross, acc, part, parts,
+    spec, src, heard, mark, picked, items, chans, base, rot, thi, tlo, mirror, cross, acc, part, parts,
     load_sem, hear_send, hear_recv, share_send, share_recv, item_send, item_recv, part_send, part_recv,
 ):
     r = lax.axis_index("recv")
@@ -75,13 +82,14 @@
         return team + 8 * (q & 1) + (q >> 1)
 
     keeps = jnp.where(w < TEAM, w, WINDOWS - 1 - w)
-    holder = r < ITEMS
+    holder = (r < SPARE) | (r == MARKER) | (r == LATE) | (r == LATE + 1)
+    mine = jnp.where(r < SPARE, r, jnp.where(r == MARKER, TILES, SPARE + r - LATE))
     own = me == keeps
     other_core = r + 1 - 2 * core
     other_chip = member(me ^ 1)
 
     loads = [
-        pltpu.make_async_copy(spec_hbm.at[0], spec.at[me], load_sem.at[0]),
+        pltpu.make_async_copy(spec_hbm.at[0], spec, load_sem.at[0]),
         pltpu.make_async_copy(src_hbm, src, load_sem.at[1]),
         pltpu.make_async_copy(base_hbm, base, load_sem.at[2]),
         pltpu.make_async_copy(rot_hbm, rot, load_sem.at[3]),
@@ -96,12 +104,8 @@
 
     @pl.when(holder)
     def _():
-        def one(i, carry):
-            step = i + RECV // 2
-            greet(lax.bitwise_and(r + jnp.where(step < RECV, step, step - RECV + 1), RECV - 1), w)
-            return carry
-
-        lax.fori_loop(0, RECV - 1, one, 0)
+        for dz, dy, dc in FAR:
+            greet((((r >> 3) + dz) & 7) * 8 + (((r >> 1) + dy) & 3) * 2 + (core ^ dc), w)
 
     greet(other_core, w)
     greet(other_chip, w)
@@ -112,47 +116,43 @@
     def _():
         greet(member(keeps), w)
 
-    def shape(cc, c):
-        both = spec[cc, c]
+    loads[0].wait()
+    for c in range(CHAN):
+        both = spec[c]
         power = jnp.sum(both * both, axis=(0, 1), keepdims=True) / BINS
         scale = jnp.broadcast_to(lax.rsqrt(power + 1e-06), (2, 128))
-        for half in range(2):
-            scales[cc, CHAN * half + c : CHAN * half + c + 1, :] = scale[0:1]
+        mark[c] = scale
+        for j in range(2):
+            chans[me, TILES, CHAN * j + c : CHAN * j + c + 1, :] = scale[0:1]
         for t in range(TILES):
-            chans[cc, t, c : c + 1, :] = both[0:1, 128 * t : 128 * t + 128]
-            chans[cc, t, CHAN + c : CHAN + c + 1, :] = both[1:2, 128 * t : 128 * t + 128]
-        return scale
-
-    loads[0].wait()
-    for c in range(CHAN):
-        mark[c] = shape(me, c)
+            chans[me, t, c : c + 1, :] = both[0:1, 128 * t : 128 * t + 128]
+            chans[me, t, CHAN + c : CHAN + c + 1, :] = both[1:2, 128 * t : 128 * t + 128]
 
     pl.semaphore_wait(barrier, ITEMS - holder.astype(jnp.int32) + WINDOWS - own.astype(jnp.int32) + 2)
 
     def tell(i, carry):
-        t = turn + lax.rem(i, FIRST_PART)
-        t = jnp.where(t < FIRST_PART, t, t - FIRST_PART) + lax.div(i, FIRST_PART) * FIRST_PART
-        piece = spec.at[me, :, :, pl.ds(pl.multiple_of(t * 128, 128), 128)]
-
-        @pl.when(t == r)
+        t = jnp.int32(SPARE + i) if i < 2 else 16 * ((i - 2) // 16) + ((r + i) & 15)
+        r2 = jnp.where(t < SPARE, t, t - SPARE + LATE)
+        piece = spec.at[:, :, pl.ds(pl.multiple_of(t * 128, 128), 128)]
+
+        @pl.when(r2 == r)
         def _():
             pltpu.make_async_copy(piece, heard.at[r], hear_recv).start()
 
-        @pl.when(t != r)
+        @pl.when(r2 != r)
         def _():
             pltpu.make_async_remote_copy(
-                piece, heard.at[r], hear_send, hear_recv, device_id=(t, w), device_id_type=MESH
+                piece, heard.at[r], hear_send, hear_recv, device_id=(r2, w), device_id_type=MESH
             ).start()
 
         return carry
 
-    turn = lax.rem(r, FIRST_PART)
     for i in range(TILES):
         tell(i, 0)
 
     def share(q, r2, sem):
         return pltpu.make_async_remote_copy(
-            spec.at[q], spec.at[q], share_send.at[sem], share_recv.at[sem], device_id=(r2, w), device_id_type=MESH
+            chans.at[q], chans.at[q], share_send.at[sem], share_recv.at[sem], device_id=(r2, w), device_id_type=MESH
         )
 
     to_chip = share(me, other_chip, 0)
@@ -175,10 +175,15 @@
     loads[3].wait()
 
     z = lax.shift_right_logical(r, 3)
-    flip = jnp.where((z >= 2) & (z <= 5), 24, 0)
+    y = (r >> 1) & 3
+    flip = jnp.where((z >= 2) & (z <= 5), 3, 0)
 
     def tile_at(p):
-        return jnp.where(p < SPARE, p ^ flip, p)
+        i = p >> 1
+        shift = 2 * (i & 7)
+        plane = ((jnp.where(i < 8, NEAR_Z[0], NEAR_Z[1]) >> shift) & 3) ^ flip
+        line = (y + ((jnp.where(i < 8, NEAR_Y[0], NEAR_Y[1]) >> shift) & 3)) & 3
+        return jnp.where(p < SPARE, (plane << 3) + (line << 1) + (p & 1), p)
 
     def table(i, carry):
         p = lax.shift_right_logical(i, 3)
@@ -195,6 +200,15 @@
 
     lax.fori_loop(0, TILES * 8, table, 0)
 
+    def mirrored(i, carry):
+        row = pl.multiple_of(i * 16, 16)
+        m = lax.broadcasted_iota(jnp.int32, (16, WIDE), 0) + row
+        j = lax.broadcasted_iota(jnp.int32, (16, WIDE), 1)
+        mirror[pl.ds(row, 16), :] = jnp.where((m + j == HALF) & (m > 0), 1.0, 0.0).astype(BF16)
+        return carry
+
+    lax.fori_loop(0, WIDE // 16, mirrored, 0)
+
     loads[1].wait()
 
     @pl.when(holder)
@@ -207,7 +221,7 @@
             q, place = min(v, WINDOWS - 1 - v), 2 * (v // TEAM) + k % 2
             picked[q, place : place + 1, :] = pair[0:1]
             picked[q, PART + place : PART + place + 1, :] = pair[1:2]
-        pltpu.make_async_copy(picked.at[me], items.at[r], item_recv.at[r]).start()
+        pltpu.make_async_copy(picked.at[me], items.at[mine], item_recv.at[mine]).start()
 
         def spread(i, carry):
             r2 = i
@@ -215,7 +229,7 @@
             @pl.when(r2 != r)
             def _():
                 pltpu.make_async_remote_copy(
-                    picked.at[member_of(i)], items.at[r], item_send, item_recv.at[r], device_id=(r2, w), device_id_type=MESH
+                    picked.at[member_of(i)], items.at[mine], item_send, item_recv.at[mine], device_id=(r2, w), device_id_type=MESH
                 ).start()
 
             return carry
@@ -225,23 +239,8 @@
 
     to_chip.wait()
     to_core_too.start()
-    for c in range(CHAN):
-        shape(me ^ 1, c)
     to_core.wait()
-    for c in range(CHAN):
-        shape(me ^ 2, c)
     to_core_too.wait()
-    for c in range(CHAN):
-        shape(me ^ 3, c)
-
-    def mirrored(i, carry):
-        row = pl.multiple_of(i * 16, 16)
-        m = lax.broadcasted_iota(jnp.int32, (16, WIDE), 0) + row
-        j = lax.broadcasted_iota(jnp.int32, (16, WIDE), 1)
-        mirror[pl.ds(row, 16), :] = jnp.where((m + j == HALF) & (m > 0), 1.0, 0.0).astype(BF16)
-        return carry
-
-    lax.fori_loop(0, WIDE // 16, mirrored, 0)
 
     x = w >> 1
     near_x = ((me >> 1) - x) & 3
@@ -294,7 +293,7 @@
             for g in range(8):
                 cc, j = g // 2, g % 2
                 scale = jnp.where(upper, items[TILES, 2 * j : 2 * j + 1, :], items[TILES, 2 * j + 1 : 2 * j + 2, :])
-                scale = scale * scales[cc]
+                scale = scale * chans[cc, TILES]
                 part[n * 8 + g] = value[8 * g : 8 * g + 8] * jnp.concatenate([scale, scale], axis=1)
             for i in range(8):
                 cc, j = me ^ (1, 3, 2, 0)[i % 4], ahead ^ (i // 4)
@@ -364,14 +363,13 @@
         in_specs=[anywhere] * 4,
         out_specs=pl.BlockSpec(memory_space=vmem),
         scratch_shapes=[
-            vmem((TEAM, CHAN, 2, BINS), F32),
+            vmem((CHAN, 2, BINS), F32),
             pltpu.SMEM((NSRC,), jnp.int32),
             vmem((RECV, CHAN, 2, 128), F32),
             vmem((CHAN, 2, 128), F32),
             vmem((TEAM, 2 * PART, 128), F32),
             vmem((RECV, 2 * PART, 128), F32),
-            vmem((TEAM, TILES, 8, 128), F32),
-            vmem((TEAM, 8, 128), F32),
+            vmem((TEAM, ITEMS, 8, 128), F32),
             vmem((256, WIDE), F32),
             vmem((TILES, 8, WIDE), F32),
             vmem((2, BINS, WIDE), BF16),

time: 40 us -> 39.7 us (level)
  no operation moved by 1% of the time
where the time goes in v5:
time: 39.7 us; the launch traced here: 39.5 us
  Pallas kernels  38.9 us (98%)
  local copies, waits for them, and re-layouts  0.62 us (2%)
    pallas_call x1, Pallas kernels, shards(): pl.pallas_call(kernel, out_shape=pltpu.VMEM((NSRC // WINDOWS, CHAN, LAGS)...  38.9 us

profile of v5, /device:TPU:1, one launch (start us, length us, event | category | flops | bytes accessed | tf_op | source)
XLA Modules:
  0.0 39.5 jit_solution(9344091082731737527)
XLA Ops:
  0.0 38.9 %shard_map.46 = f32[2,4,1001]{2,1,0:T(4,128)S(1)} custom-call(f32[1,4,2,4352]{3,2,1,0:T(2,128)} %spec_hbm.1, s32[16]{0:T(128)} %src_hbm.1, f32[256,512]{1,0:T(8,128)} %constant.4.clone.base_hbm, f32[34,8,512]{2,1,0:T(8,128)} %constant.5.clone.rot_hbm), custom_call_target="tpu_custom_call" | custom-call | tf_op jit(solution)/shard_map/pallas_call | solution.py:360
  38.9 0.6 %copy.6 = f32[2,4,1001]{2,1,0:T(4,128)} copy(f32[2,4,1001]{2,1,0:T(4,128)S(1)} %shard_map.46) | data formatting | bytes 64064

commit v6 on v5

--- a/solution.py
+++ b/solution.py
@@ -294,32 +294,37 @@
                 cc, j = g // 2, g % 2
                 scale = jnp.where(upper, items[TILES, 2 * j : 2 * j + 1, :], items[TILES, 2 * j + 1 : 2 * j + 2, :])
                 scale = scale * chans[cc, TILES]
-                part[n * 8 + g] = value[8 * g : 8 * g + 8] * jnp.concatenate([scale, scale], axis=1)
+                part[n // 2 * 8 + g, :, CUT * (n % 2) : CUT * (n % 2) + CUT] = value[8 * g : 8 * g + 8] * jnp.concatenate(
+                    [scale, scale], axis=1
+                )
+            if n % 2 == 0:
+                continue
+            h = n // 2
             for i in range(8):
                 cc, j = me ^ (1, 3, 2, 0)[i % 4], ahead ^ (i // 4)
                 r2, w2 = member(cc), jnp.where(j == 0, me, WINDOWS - 1 - me)
-                g = n * 8 + cc * 2 + j
+                g = h * 8 + cc * 2 + j
                 self = (r2 == r) & (w2 == w)
 
                 @pl.when(self)
-                def _(n=n, g=g):
-                    pltpu.make_async_copy(part.at[g], parts.at[n, w], part_recv.at[n]).start()
+                def _(h=h, g=g):
+                    pltpu.make_async_copy(part.at[g], parts.at[h, w], part_recv.at[h]).start()
 
                 @pl.when(jnp.logical_not(self))
-                def _(n=n, g=g, r2=r2, w2=w2):
+                def _(h=h, g=g, r2=r2, w2=w2):
                     pltpu.make_async_remote_copy(
-                        part.at[g], parts.at[n, w], part_send, part_recv.at[n], device_id=(r2, w2), device_id_type=MESH
+                        part.at[g], parts.at[h, w], part_send, part_recv.at[h], device_id=(r2, w2), device_id_type=MESH
                     ).start()
 
     total = []
-    for n in range(4):
-        pltpu.make_async_copy(parts.at[n], parts.at[n], part_recv.at[n]).wait()
-        value = parts[n, 0]
+    for h in range(2):
+        pltpu.make_async_copy(parts.at[h], parts.at[h], part_recv.at[h]).wait()
+        value = parts[h, 0]
         for v in range(1, WINDOWS):
-            value = value + parts[n, v]
+            value = value + parts[h, v]
         total.append(value)
-    even = jnp.concatenate(total[0::2], axis=1)
-    odd = jnp.concatenate(total[1::2], axis=1)
+    even = jnp.concatenate([value[:, 0:CUT] for value in total], axis=1)
+    odd = jnp.concatenate([value[:, CUT:] for value in total], axis=1)
     before = even + odd
     one = before.astype(BF16)
     rest = before - one.astype(F32)
@@ -345,7 +350,7 @@
 
     @pl.when(own)
     def _():
-        pltpu.make_async_copy(part.at[pl.ds(0, 28)], part.at[pl.ds(0, 28)], part_send).wait()
+        pltpu.make_async_copy(part.at[pl.ds(0, 14)], part.at[pl.ds(0, 14)], part_send).wait()
 
     @pl.when(jnp.logical_not(own))
     def _():
@@ -377,8 +382,8 @@
             vmem((WIDE, WIDE), BF16),
             vmem((2, 128, BINS), BF16),
             vmem((4, 64, CUT), F32),
-            vmem((32, 8, CUT), F32),
-            vmem((4, WINDOWS, 8, CUT), F32),
+            vmem((16, 8, 2 * CUT), F32),
+            vmem((2, WINDOWS, 8, 2 * CUT), F32),
             dma((4,)),
             dma,
             dma,
@@ -387,7 +392,7 @@
             dma,
             dma((ITEMS,)),
             dma,
-            dma((4,)),
+            dma((2,)),
         ],
         compiler_params=pltpu.CompilerParams(
             collective_id=0, has_side_effects=True, vmem_limit_bytes=60 * 1024 * 1024

time: 39.7 us -> 39.5 us (level)
  no operation moved by 1% of the time
where the time goes in v6:
time: 39.5 us; the launch traced here: 39.4 us
  Pallas kernels  38.8 us (98%)
  local copies, waits for them, and re-layouts  0.62 us (2%)
    pallas_call x1, Pallas kernels, shards(): pl.pallas_call(kernel, out_shape=pltpu.VMEM((NSRC // WINDOWS, CHAN, LAGS)...  38.8 us

profile of v6, /device:TPU:1, one launch (start us, length us, event | category | flops | bytes accessed | tf_op | source)
XLA Modules:
  0.0 39.4 jit_solution(12517178586662746489)
XLA Ops:
  0.0 38.8 %shard_map.46 = f32[2,4,1001]{2,1,0:T(4,128)S(1)} custom-call(f32[1,4,2,4352]{3,2,1,0:T(2,128)} %spec_hbm.1, s32[16]{0:T(128)} %src_hbm.1, f32[256,512]{1,0:T(8,128)} %constant.4.clone.base_hbm, f32[34,8,512]{2,1,0:T(8,128)} %constant.5.clone.rot_hbm), custom_call_target="tpu_custom_call" | custom-call | tf_op jit(solution)/shard_map/pallas_call | solution.py:365
  38.8 0.6 %copy.6 = f32[2,4,1001]{2,1,0:T(4,128)} copy(f32[2,4,1001]{2,1,0:T(4,128)S(1)} %shard_map.46) | data formatting | bytes 64064
